TPU v7x, 512 devices: a whole 4x8x8 slice. The times are simulated.
512 devices in a mesh: blk: 8 (over y), uly: 8 (over x, core), tp: 8 (over z).
Axes of the slice: x: 4, y: 8, z: 8, core: 2. Of those that a mesh axis runs over, the one named last changes fastest.
Arguments:
- queries: bfloat16 [8192, 64, 128], P(('blk', 'uly'), 'tp'), may hold values from -84 to 84
- keys: bfloat16 [8192, 8, 128], P(('blk', 'uly'), 'tp'), may hold values from -12 to 12
- values: bfloat16 [8192, 8, 128], P(('blk', 'uly'), 'tp'), may hold values from -6 to 6
- span_order: int32 [16], replicated, may hold values from 0 to 15, each once
Outputs:
- attended: bfloat16 [8192, 64, 128], P(('blk', 'uly'), 'tp')
Inputs may be any that keep to these rules, and one draw needn't show every extreme that they name: `span_order`: holds every number from 0 to 15 exactly once.
All inputs are finite; a program needn't handle non-finite values.
Results may differ from a plain program's by a relative error of at most 0.0065.
Values may be sent and summed in bfloat16 or wider, within the bound.
No kernel may reach another device: no remote copies, remote signals or barrier semaphores. Data moves between devices by JAX's collectives and lax.ppermute only.
A program may use at most 64 MiB of HBM per device.

v0:
```python
import math
import jax
import jax.numpy as jnp
from jax import lax
from jax.sharding import PartitionSpec as P


def span_positions(row_index, span_order, span_len):
    span_index = row_index // span_len
    span_ids = jnp.arange(span_order.shape[0], dtype=jnp.int32)
    span_hit = span_index[:, None] == span_ids[None, :]
    start_pos = jnp.sum(jnp.where(span_hit, span_order[None, :], 0), axis=1)
    return start_pos * span_len + row_index % span_len


def attend_block(carry_state, query_four, query_pos, key_block, value_block, key_pos, score_scale):
    running_max, running_sum, weighted = carry_state
    scores = (
        jnp.einsum("rhgd,phd->rhgp", query_four, key_block, preferred_element_type=jnp.float32)
        * score_scale
    )
    visible = (key_pos[None, :] <= query_pos[:, None])[:, None, None, :]
    scores = jnp.where(visible, scores, -1e30)
    next_max = jnp.maximum(running_max, jnp.max(scores, axis=3))
    weights = jnp.where(visible, jnp.exp(scores - next_max[..., None]), 0.0)
    rescale = jnp.exp(running_max - next_max)
    running_sum = running_sum * rescale + jnp.sum(weights, axis=3)
    weighted = weighted * rescale[..., None] + jnp.einsum(
        "rhgp,phd->rhgd",
        weights.astype(jnp.bfloat16),
        value_block,
        preferred_element_type=jnp.float32,
    )
    return (next_max, running_sum, weighted)


def make_folder(query_four, query_pos, span_order, span_len):
    score_scale = 1.0 / math.sqrt(query_four.shape[3])

    def fold_keys(carry_state, key_piece, start):
        piece_keys, piece_values = key_piece
        piece_rows = piece_keys.shape[0]
        block_rows = 512
        block_count = piece_rows // block_rows
        heads_here = piece_keys.shape[1]
        head_size = piece_keys.shape[2]
        key_blocks = piece_keys.reshape(block_count, block_rows, heads_here, head_size)
        value_blocks = piece_values.reshape(block_count, block_rows, heads_here, head_size)
        key_positions = span_positions(
            jnp.arange(piece_rows, dtype=jnp.int32), span_order, span_len
        )
        key_positions = key_positions.reshape(block_count, block_rows)

        def scan_step(inner_state, block_item):
            key_block, value_block, key_pos = block_item
            inner_state = attend_block(
                inner_state, query_four, query_pos, key_block, value_block, key_pos, score_scale
            )
            return (inner_state, None)

        carry_state, _ = lax.scan(scan_step, carry_state, (key_blocks, value_blocks, key_positions))
        return carry_state

    return fold_keys


def initial_state(query_four):
    lead_shape = query_four.shape[:3]
    return (
        jnp.full(lead_shape, -1e30, jnp.float32),
        jnp.zeros(lead_shape, jnp.float32),
        jnp.zeros(query_four.shape, jnp.float32),
    )


def finish_state(final_state):
    running_max, running_sum, weighted = final_state
    return (weighted / running_sum[..., None]).astype(jnp.bfloat16)


def local(queries, keys, values, span_order):
    tok_rows = queries.shape[0]
    head_size = queries.shape[2]
    uly_size = lax.axis_size("uly")
    span_len = tok_rows * uly_size // 2
    blk_place = lax.axis_index("blk")
    query_heads = lax.all_to_all(queries, "uly", split_axis=1, concat_axis=0, tiled=True)
    local_rows = query_heads.shape[0]
    per_device = query_heads.shape[1]
    query_four = query_heads.reshape(local_rows, 1, per_device, head_size)
    query_pos = span_positions(
        blk_place * local_rows + jnp.arange(local_rows, dtype=jnp.int32), span_order, span_len
    )
    folder = make_folder(query_four, query_pos, span_order, span_len)
    final_state = folder(
        initial_state(query_four),
        (
            lax.all_gather(keys, ("blk", "uly"), axis=0, tiled=True),
            lax.all_gather(values, ("blk", "uly"), axis=0, tiled=True),
        ),
        jnp.int32(0),
    )
    head_output = finish_state(final_state).reshape(local_rows, per_device, head_size)
    return lax.all_to_all(head_output, "uly", split_axis=0, concat_axis=1, tiled=True)


def solution(mesh):
    in_specs = (
        P(("blk", "uly"), "tp", None),
        P(("blk", "uly"), "tp", None),
        P(("blk", "uly"), "tp", None),
        P(),
    )
    out_specs = P(("blk", "uly"), "tp", None)
    return jax.shard_map(local, mesh=mesh, in_specs=in_specs, out_specs=out_specs, check_vma=False)
```

profile of v0, /device:TPU:1, one launch (start us, length us, event | category | flops | bytes accessed | tf_op | source)
XLA Modules:
  0.0 263.5 jit_solution(8121300190383267117)
XLA Ops:
  8.0 1.7 copy.22
  9.7 10.2 %all-to-all-start = ((bf16[128,8,128]{2,0,1:T(8,128)(2,1)}), bf16[128,8,128]{2,0,1:T(8,128)(2,1)S(1)}, u32[]{:S(2)}, u32[]{:S(2)}) async-start(bf16[128,8,128]{2,0,1:T(8,128)(2,1)} %copy.22), calls=%async_computation | async-start | bytes 524288 | tf_op jit(solution)/shard_map/all_to_all | solution.py:87
  21.6 4.8 %all-to-all-done = bf16[128,8,128]{2,0,1:T(8,128)(2,1)S(1)} async-done(((bf16[128,8,128]{2,0,1:T(8,128)(2,1)}), bf16[128,8,128]{2,0,1:T(8,128)(2,1)S(1)}, u32[]{:S(2)}, u32[]{:S(2)}) %all-to-all-start) | async-done | bytes 262176 | tf_op jit(solution)/shard_map/all_to_all | solution.py:87
  26.4 72.7 %all-gather.3.cloned.1.call-done = bf16[8192,1,128]{2,0,1:T(8,128)(2,1)} async-done(((bf16[128,1,128]{2,0,1:T(8,128)(2,1)}), bf16[8192,1,128]{2,0,1:T(8,128)(2,1)}) %all-gather.3.cloned.1.call-update) | async-done | bytes 2097168 | tf_op jit(solution)/shard_map/all_gather | solution.py:98
  99.1 83.9 %all-gather.5.cloned.1.call-done = bf16[8192,1,128]{2,0,1:T(8,128)(2,1)} async-done(((bf16[128,1,128]{2,0,1:T(8,128)(2,1)}), bf16[8192,1,128]{2,0,1:T(8,128)(2,1)}) %all-gather.5.cloned.1.call-update) | async-done | bytes 2097168 | tf_op jit(solution)/shard_map/all_gather | solution.py:99
  183.0 60.9 %while.15 = (s32[]{:T(128)}, f32[1024,1,1]{0,2,1:T(1,128)S(1)}, f32[1024,1,1]{0,2,1:T(1,128)S(1)}, f32[1024,1,1,128]{0,3,2,1:T(8,128)S(1)}, s32[16,512]{1,0:T(8,...) while((s32[]{:T(128)}, f32[1024,1,1]{0,2,1:T(1,128)S(1)}, ...), condition=%wide.region_5.6_spmd.clone, body=%wide.region_2.5_spmd.clone.sunk | while | flops 277222400 | bytes 7953533 | solution.py:61
  183.0 1.4 fusion.47
  185.0 1.7 fusion.51
  186.8 1.4 fusion.47
  188.8 1.7 fusion.51
  190.6 1.4 fusion.47
  192.7 1.7 fusion.51
  196.5 1.7 fusion.51
  198.2 1.4 fusion.47
  200.3 1.7 fusion.51
  204.1 1.7 fusion.51
  205.8 1.4 fusion.47
  207.9 1.7 fusion.51
  211.7 1.7 fusion.51
  213.4 1.4 fusion.47
  215.5 1.7 fusion.51
  219.3 1.7 fusion.51
  221.0 1.4 fusion.47
  223.1 1.7 fusion.51
  226.9 1.7 fusion.51
  228.7 1.4 fusion.47
  230.7 1.7 fusion.51
  234.5 1.7 fusion.51
  236.3 1.4 fusion.47
  238.3 1.7 fusion.51
  242.1 1.7 fusion.51
  245.7 9.8 %all_to_all.33 = bf16[8,2,8192]{2,1,0:T(2,128)(2,1)S(1)} all-to-all(bf16[8,2,8192]{2,1,0:T(2,128)(2,1)S(1)} %reshape.133), channel_id=1, replica_groups=mesh['blk'=8,'uly'=8,'tp'=8] {'uly'}, dimensions={0} | all-to-all | bytes 524288 | tf_op jit(solution)/shard_map/all_to_all | solution.py:104
  (110 shorter events, 26.4 us)
Async XLA Ops:
  6.5 92.5 %all-gather.3.cloned.1.call-start = ((), (), s32[]{:S(2)}) async-start(), calls=%async_computation.2 | async-start | bytes 2129920 | tf_op jit(solution)/shard_map/all_gather | solution.py:98
  7.3 175.7 %all-gather.5.cloned.1.call-start = ((), (), s32[]{:S(2)}) async-start(), calls=%async_computation.3 | async-start | bytes 2129920 | tf_op jit(solution)/shard_map/all_gather | solution.py:99
  9.7 16.7 %all-to-all-start = ((bf16[128,8,128]{2,0,1:T(8,128)(2,1)}), bf16[128,8,128]{2,0,1:T(8,128)(2,1)S(1)}, u32[]{:S(2)}, u32[]{:S(2)}) async-start(bf16[128,8,128]{2,0,1:T(8,128)(2,1)} %copy.22), calls=%async_computation | async-start | bytes 524288 | tf_op jit(solution)/shard_map/all_to_all | solution.py:87
Sparse Core Ops, SparseCore 0:
  10.7 88.3 all-gather.2
  102.4 80.5 all-gather.4
where the time goes:
time: 264 us; the launch traced here: 263 us
  waiting for transfers between devices  163 us (62%)
  matrix products  49 us (19%)
  between operations  13.5 us (5%)
  other arithmetic  13.2 us (5%)
  starting transfers between devices  10.2 us (4%)
  blocking collectives  9.79 us (4%)
  local copies, waits for them, and re-layouts  3.84 us (1%)
    all_gather x1, waiting for transfers between devices, local(): lax.all_gather(values, ('blk', 'uly'), axis=0, tiled=True)  83.9 us
    all_gather x1, waiting for transfers between devices, local(): lax.all_gather(keys, ('blk', 'uly'), axis=0, tiled=True)  72.7 us
    dot_general x16, matrix products, attend_block(): jnp.einsum('rhgp,phd->rhgd', weights.astype(jnp.bfloat16), value_block, p...  27.1 us
    dot_general x16, matrix products, attend_block(): jnp.einsum('rhgd,phd->rhgp', query_four, key_block, preferred_element_typ...  21.9 us
    all_to_all x1, starting transfers between devices, local(): lax.all_to_all(queries, 'uly', split_axis=1, concat_axis=0, tiled=True)  10.2 us
    reduce_sum x16, other arithmetic, attend_block(): running_sum = running_sum * rescale + jnp.sum(weights, axis=3)  9.98 us
    all_to_all x1, blocking collectives, local(): lax.all_to_all(head_output, 'uly', split_axis=0, concat_axis=1, tiled=True)  9.79 us
  transfers between devices with their start and end apart: 3, of which 3 were waited for; matrix products, arithmetic and copies ran while one was open for 1% of the time, Pallas kernels for 0%

commit v1 on v0

--- a/solution.py
+++ b/solution.py
@@ -3,6 +3,13 @@
 import jax.numpy as jnp
 from jax import lax
 from jax.sharding import PartitionSpec as P
+
+
+def swapped_in(block, mesh_axis, dim):
+    size = lax.axis_size(mesh_axis)
+    blocks = jnp.stack([block for _ in range(size)])
+    blocks = lax.all_to_all(blocks, mesh_axis, split_axis=0, concat_axis=0)
+    return jnp.concatenate(blocks, axis=dim)
 
 
 def span_positions(row_index, span_order, span_len):
@@ -96,7 +103,7 @@
         initial_state(query_four),
         (
             lax.all_gather(keys, ("blk", "uly"), axis=0, tiled=True),
-            lax.all_gather(values, ("blk", "uly"), axis=0, tiled=True),
+            swapped_in(values, ("blk", "uly"), 0),
         ),
         jnp.int32(0),
     )

time: 264 us -> 207 us (0.78)
  waiting for transfers between devices: 163 us -> 93.5 us
  blocking collectives: 9.79 us -> 25.6 us
  starting transfers between devices: 10.2 us -> 6.13 us
    all_gather x1 -> x0, waiting for transfers between devices: 83.9 us -> none  [local(): lax.all_gather(values, ('blk', 'uly'), axis=0, tiled=True)]
    all_to_all x1, waiting for transfers between devices: 4.82 us -> 50 us  [swapped_in(): blocks = lax.all_to_all(blocks, mesh_axis, split_axis=0, concat_axis=0)]
    all_gather x1, waiting for transfers between devices: 72.7 us -> 42.8 us  [local(): lax.all_gather(keys, ('blk', 'uly'), axis=0, tiled=True)]
    all_to_all x0 -> x1, blocking collectives: none -> 15.8 us  [local(): lax.all_to_all(queries, 'uly', split_axis=1, concat_axis=0, tiled=True)]
    all_to_all x1, starting transfers between devices: 10.2 us -> 6.09 us  [swapped_in(): blocks = lax.all_to_all(blocks, mesh_axis, split_axis=0, concat_axis=0)]
  transfers between devices with their start and end apart: 3 -> 2, of which waited for: 3 -> 2; matrix products, arithmetic and copies ran while one was open for 1% -> 0% of each run, Pallas kernels for 0% -> 0%
where the time goes in v1:
time: 207 us; the launch traced here: 206 us
  waiting for transfers between devices  93.5 us (45%)
  matrix products  49 us (24%)
  blocking collectives  25.6 us (12%)
  between operations  13.5 us (7%)
  other arithmetic  11.9 us (6%)
  starting transfers between devices  6.13 us (3%)
  local copies, waits for them, and re-layouts  5.73 us (3%)
    all_to_all x1, waiting for transfers between devices, swapped_in(): blocks = lax.all_to_all(blocks, mesh_axis, split_axis=0, concat_axis=0)  50 us
    all_gather x1, waiting for transfers between devices, local(): lax.all_gather(keys, ('blk', 'uly'), axis=0, tiled=True)  42.8 us
    dot_general x16, matrix products, attend_block(): jnp.einsum('rhgp,phd->rhgd', weights.astype(jnp.bfloat16), value_block, p...  27.1 us
    dot_general x16, matrix products, attend_block(): jnp.einsum('rhgd,phd->rhgp', query_four, key_block, preferred_element_typ...  21.8 us
    all_to_all x1, blocking collectives, local(): lax.all_to_all(queries, 'uly', split_axis=1, concat_axis=0, tiled=True)  15.8 us
    reduce_sum x16, other arithmetic, attend_block(): running_sum = running_sum * rescale + jnp.sum(weights, axis=3)  9.98 us
    all_to_all x1, blocking collectives, local(): lax.all_to_all(head_output, 'uly', split_axis=0, concat_axis=1, tiled=True)  9.79 us
    all_to_all x1, starting transfers between devices, swapped_in(): blocks = lax.all_to_all(blocks, mesh_axis, split_axis=0, concat_axis=0)  6.09 us
  transfers between devices with their start and end apart: 2, of which 2 were waited for; matrix products, arithmetic and copies ran while one was open for 0% of the time, Pallas kernels for 0%

profile of v1, /device:TPU:1, one launch (start us, length us, event | category | flops | bytes accessed | tf_op | source)
XLA Modules:
  0.0 206.5 jit_solution(14951483224175524179)
XLA Ops:
  7.5 15.8 %all_to_all.38 = bf16[128,8,128]{2,0,1:T(8,128)(2,1)S(1)} all-to-all(bf16[128,8,128]{2,0,1:T(8,128)(2,1)S(1)} %copy.22), channel_id=1, replica_groups=mesh['blk'=8,'uly'=8,'tp'=8] {'uly'}, dimensions={1} | all-to-all | bytes 524288 | tf_op jit(solution)/shard_map/all_to_all | solution.py:94
  23.3 2.6 %stack.2 = bf16[64,128,1,128]{3,1,2,0:T(8,128)(2,1)} broadcast(bf16[128,128]{1,0:T(8,128)(2,1)} %bitcast.99), dimensions={1,3} | broadcast | bytes 2129920 | tf_op jit(solution)/shard_map/stack | solution.py:10
  25.9 6.1 %all-to-all-start.1 = ((bf16[64,128,1,128]{3,1,2,0:T(8,128)(2,1)}), bf16[64,128,1,128]{3,1,2,0:T(8,128)(2,1)}, u32[]{:S(2)}, u32[]{:S(2)}) async-start(bf16[64,128,1,128]{3,1,2,0:T(8,128)(2,1)} %stack.2), calls=%async_computation.1 | async-start | bytes 4194304 | tf_op jit(solution)/shard_map/all_to_all | solution.py:11
  33.2 50.0 %all-to-all-done.1 = bf16[64,128,1,128]{3,1,2,0:T(8,128)(2,1)} async-done(((bf16[64,128,1,128]{3,1,2,0:T(8,128)(2,1)}), bf16[64,128,1,128]{3,1,2,0:T(8,128)(2,1)}, u32[]{:S(2)}, u32[]{:S(2)}) %all-to-all-start.1) | async-done | bytes 2097184 | tf_op jit(solution)/shard_map/all_to_all | solution.py:11
  83.2 42.8 %all-gather.2.cloned.1.call-done = bf16[8192,1,128]{2,0,1:T(8,128)(2,1)} async-done(((bf16[128,1,128]{2,0,1:T(8,128)(2,1)}), bf16[8192,1,128]{2,0,1:T(8,128)(2,1)}) %all-gather.2.cloned.1.call-update) | async-done | bytes 2097168 | tf_op jit(solution)/shard_map/all_gather | solution.py:105
  126.0 60.8 %while.15 = (s32[]{:T(128)}, f32[1024,1,1]{0,2,1:T(1,128)S(1)}, f32[1024,1,1]{0,2,1:T(1,128)S(1)}, f32[1024,1,1,128]{0,3,2,1:T(8,128)S(1)}, s32[16,512]{1,0:T(8,...) while((s32[]{:T(128)}, f32[1024,1,1]{0,2,1:T(1,128)S(1)}, ...), condition=%wide.region_5.6_spmd.clone, body=%wide.region_2.5_spmd.clone.sunk | while | flops 277222400 | bytes 7953533 | solution.py:68
  128.1 1.7 fusion.51
  129.8 1.4 fusion.47
  131.9 1.7 fusion.51
  133.6 1.4 fusion.47
  135.7 1.7 fusion.51
  137.4 1.4 fusion.47
  139.5 1.7 fusion.51
  143.3 1.7 fusion.51
  145.0 1.4 fusion.47
  147.1 1.7 fusion.51
  150.9 1.7 fusion.51
  152.6 1.4 fusion.47
  154.7 1.7 fusion.51
  158.5 1.7 fusion.51
  160.2 1.4 fusion.47
  162.3 1.7 fusion.51
  166.1 1.7 fusion.51
  167.8 1.4 fusion.47
  169.9 1.7 fusion.51
  173.7 1.7 fusion.51
  175.4 1.4 fusion.47
  177.5 1.7 fusion.51
  181.3 1.7 fusion.51
  183.0 1.4 fusion.47
  185.1 1.7 fusion.51
  188.6 9.8 %all_to_all.39 = bf16[8,2,8192]{2,1,0:T(2,128)(2,1)S(1)} all-to-all(bf16[8,2,8192]{2,1,0:T(2,128)(2,1)S(1)} %reshape.132), channel_id=1, replica_groups=mesh['blk'=8,'uly'=8,'tp'=8] {'uly'}, dimensions={0} | all-to-all | bytes 524288 | tf_op jit(solution)/shard_map/all_to_all | solution.py:111
  (111 shorter events, 25.3 us)
Async XLA Ops:
  25.9 6.9 %copy-start = (s32[16]{0:T(128)S(1)}, s32[16]{0:T(128)}, u32[]{:S(2)}) copy-start(s32[16]{0:T(128)} %param.9) | copy-start | bytes 196
  25.9 57.3 %all-to-all-start.1 = ((bf16[64,128,1,128]{3,1,2,0:T(8,128)(2,1)}), bf16[64,128,1,128]{3,1,2,0:T(8,128)(2,1)}, u32[]{:S(2)}, u32[]{:S(2)}) async-start(bf16[64,128,1,128]{3,1,2,0:T(8,128)(2,1)} %stack.2), calls=%async_computation.1 | async-start | bytes 4194304 | tf_op jit(solution)/shard_map/all_to_all | solution.py:11
  32.0 94.0 %all-gather.2.cloned.1.call-start = ((), (), s32[]{:S(2)}) async-start(), calls=%async_computation.3 | async-start | bytes 2129920 | tf_op jit(solution)/shard_map/all_gather | solution.py:105
Sparse Core Ops, SparseCore 0:
  36.2 89.7 all-gather.1
